TPU v7x, 512 devices: a whole 4x8x8 slice. The times are simulated.
512 devices in a mesh: row: 16 (over z, core), col: 32 (over y, x).
Axes of the slice: x: 4, y: 8, z: 8, core: 2. Of those that a mesh axis runs over, the one named last changes fastest.
Arguments:
- train_embed: bfloat16 [8192, 256], P(('row', 'col')), may hold values from -16 to 16
- valid_embed: bfloat16 [65536, 256], P(('row', 'col')), may hold values from -16 to 16
- train_labels: int32 [8192], P(('row', 'col')), may hold values from 0 to 99
- valid_labels: int32 [65536], P(('row', 'col')), may hold values from 0 to 99
- pair_level: int32 [100, 100], replicated, may hold values from 0 to 3
- level_cost: float32 [4], replicated, may hold values from 0.05 to 1
Outputs:
- calibrated: float32 [8192], P('row')
All inputs are finite; a program needn't handle non-finite values.
Results may differ from a plain program's by a relative error of at most 0.0003.
Values may be sent and summed in bfloat16 or wider, within the bound.
No kernel may reach another device: no remote copies, remote signals or barrier semaphores. Data moves between devices by JAX's collectives and lax.ppermute only.
A program may use at most 64 MiB of HBM per device.

v0:
```python
import math
import jax
import jax.numpy as jnp
from jax import lax
from jax.sharding import PartitionSpec as P

ITERS = 4
entropy_scale = 0.05


def inner_products(left_rows, right_rows):
    return lax.dot_general(
        left_rows, right_rows, (((1,), (1,)), ((), ())), preferred_element_type=jnp.float32
    )


def squared_norms(embeddings):
    widened = embeddings.astype(jnp.float32)
    return jnp.sum(widened * widened, axis=1)


def class_costs(pair_level, level_cost):
    num_levels = level_cost.shape[0]
    selected = (
        pair_level[:, :, None] == jnp.arange(num_levels, dtype=jnp.int32)[None, None, :]
    ).astype(jnp.float32)
    return jnp.sum(selected * level_cost[None, None, :], axis=2)


def label_costs(row_labels, class_ids, labels_y):
    col_hot = (class_ids[:, None] == labels_y[None, :]).astype(jnp.float32)
    return jnp.dot(
        row_labels, col_hot, precision=lax.Precision.HIGHEST, preferred_element_type=jnp.float32
    )


def shards(train_embed, valid_embed, train_labels, valid_labels, pair_level, level_cost):
    rows_x, labels_x = (
        lax.all_gather(train_embed, "col", axis=0, tiled=True),
        lax.all_gather(train_labels, "col", axis=0, tiled=True),
    )
    width_d = rows_x.shape[1]
    classes = pair_level.shape[0]
    class_table = class_costs(pair_level, level_cost)
    class_ids = jnp.arange(classes, dtype=jnp.int32)
    train_hot = (labels_x[:, None] == class_ids[None, :]).astype(jnp.float32)
    row_labels = jnp.dot(
        train_hot, class_table, precision=lax.Precision.HIGHEST, preferred_element_type=jnp.float32
    )
    train_sq = squared_norms(rows_x)
    cols_y, labels_y = (
        lax.all_gather(valid_embed, "row", axis=0, tiled=True),
        lax.all_gather(valid_labels, "row", axis=0, tiled=True),
    )
    valid_sq = squared_norms(cols_y)
    label_full = label_costs(row_labels, class_ids, labels_y)

    def cost_block(offset, block_cols):
        block_y = lax.dynamic_slice_in_dim(cols_y, offset, block_cols, 0)
        block_sq = lax.dynamic_slice_in_dim(valid_sq, offset, block_cols, 0)
        label_slice = lax.dynamic_slice_in_dim(label_full, offset, block_cols, 1)
        return (
            train_sq[:, None] + block_sq[None, :] - 2.0 * inner_products(rows_x, block_y)
        ) / width_d + label_slice

    row_count = rows_x.shape[0]
    col_count = labels_y.shape[0]
    block_cols = min(512, col_count)
    block_count = col_count // block_cols
    block_ids = jnp.arange(block_count, dtype=jnp.int32)

    def scores(block_index, row_pot, col_pot):
        offset = block_index * block_cols
        cost_tile = cost_block(offset, block_cols)
        block_pot = lax.dynamic_slice_in_dim(col_pot, offset, block_cols, 0)
        return (
            (block_pot[None, :] - cost_tile) / entropy_scale,
            (row_pot[:, None] - cost_tile) / entropy_scale,
        )

    row_pot = jnp.zeros((row_count,), jnp.float32)
    col_pot = jnp.zeros((col_count,), jnp.float32)
    full_rows = row_count * lax.axis_size("row")
    full_cols = col_count * lax.axis_size("col")
    for iteration in range(ITERS):

        def local_peaks(running, block_index, row_pot=row_pot, col_pot=col_pot):
            row_side, col_side = scores(block_index, row_pot, col_pot)
            return (jnp.maximum(running, jnp.max(row_side, axis=1)), jnp.max(col_side, axis=0))

        row_local, col_local = lax.scan(
            local_peaks, jnp.full((row_count,), -jnp.inf, jnp.float32), block_ids
        )
        row_high = lax.pmax(row_local, "col")
        col_high = lax.pmax(col_local.reshape(col_count), "row")

        def local_totals(
            running,
            block_index,
            row_pot=row_pot,
            col_pot=col_pot,
            row_high=row_high,
            col_high=col_high,
        ):
            row_side, col_side = scores(block_index, row_pot, col_pot)
            block_high = lax.dynamic_slice_in_dim(col_high, block_index * block_cols, block_cols, 0)
            return (
                running + jnp.sum(jnp.exp(row_side - row_high[:, None]), axis=1),
                jnp.sum(jnp.exp(col_side - block_high[None, :]), axis=0),
            )

        row_part, col_part = lax.scan(local_totals, jnp.zeros((row_count,), jnp.float32), block_ids)
        row_sum = lax.psum(row_part, "col")
        col_sum = lax.psum(col_part.reshape(col_count), "row")
        row_new = entropy_scale * math.log(full_cols) - entropy_scale * (
            row_high + jnp.log(row_sum)
        )
        col_new = entropy_scale * math.log(full_rows) - entropy_scale * (
            col_high + jnp.log(col_sum)
        )
        row_pot = 0.5 * (row_pot + row_new)
        col_pot = 0.5 * (col_pot + col_new)
    potential_sum = lax.psum(jnp.sum(row_pot), "row")
    return (row_pot * full_rows - potential_sum) / (full_rows - 1)


def solution(mesh):
    placed = (
        P(("row", "col"), None),
        P(("row", "col"), None),
        P(("row", "col")),
        P(("row", "col")),
        P(),
        P(),
    )
    return jax.shard_map(shards, mesh=mesh, in_specs=placed, out_specs=P("row"), check_vma=False)
```

profile of v0, /device:TPU:1, one launch (start us, length us, event | category | flops | bytes accessed | tf_op | source)
XLA Modules:
  0.0 894.9 jit_solution(5116224132933514768)
XLA Ops:
  10.3 17.5 %all-reduce = s32[512]{0:T(512)S(1)} all-reduce(s32[512]{0:T(512)S(1)} %dynamic-update-slice), channel_id=1, replica_groups=mesh['row'=16,'col'=32] {'col'}, use_global_device_ids=true, to_apply=%add | all-reduce | flops 512 | bytes 4096
  27.7 28.0 %all-gather = s32[16,1,128]{2,1,0:T(1,128)S(1)} all-gather(s32[1,1,128]{2,1,0:T(1,128)} %bitcast.194), channel_id=1, replica_groups=mesh['row'=16,'col'=32] {'row'}, dimensions={0}, use_global_device_ids=true | all-gather | bytes 8704 | tf_op jit(solution)/shard_map/all_gather | solution.py:53
  55.7 34.7 %all_gather.12 = bf16[512,256]{1,0:T(8,128)(2,1)S(1)} all-gather(bf16[16,256]{1,0:T(8,128)(2,1)} %param.22), channel_id=1, replica_groups=mesh['row'=16,'col'=32] {'col'}, dimensions={0}, use_global_device_ids=true | all-gather | bytes 270336 | tf_op jit(solution)/shard_map/all_gather | solution.py:39
  97.4 13.7 %while.100 = (s32[]{:T(128)}, f32[512]{0:T(512)S(1)}, f32[4,512]{1,0:T(4,128)S(1)}, f32[512]{0:T(512)S(1)}, s32[4]{0:T(128)S(1)}, /*index=5*/f32[2048]{0:T(1024)...) while((s32[]{:T(128)}, f32[512]{0:T(512)S(1)}, ...), condition=%wide.region_6.7_spmd.clone, body=%wide.region_3.6_spmd.clone.sunk | while | flops 136577024 | bytes 1596617 | solution.py:91
  111.1 36.0 %pmax.50 = f32[2048]{0:T(1024)S(1)} all-reduce(f32[2048]{0:T(1024)S(1)} %bitcast.188), channel_id=1, replica_groups=mesh['row'=16,'col'=32] {'row'}, use_global_device_ids=true, to_apply=%region_8.9 | all-reduce | flops 2048 | bytes 16384 | tf_op jit(solution)/shard_map/pmax | solution.py:95
  147.1 58.1 %pmax.49 = f32[512]{0:T(512)S(1)} all-reduce(f32[512]{0:T(512)S(1)} %get-tuple-element.462), channel_id=1, replica_groups=mesh['row'=16,'col'=32] {'col'}, use_global_device_ids=true, to_apply=%region_7.8 | all-reduce | flops 512 | bytes 4096 | tf_op jit(solution)/shard_map/pmax | solution.py:94
  205.2 14.1 %while.101 = (s32[]{:T(128)}, f32[512]{0:T(512)S(1)}, f32[4,512]{1,0:T(4,128)S(1)}, f32[512]{0:T(512)S(1)}, s32[4]{0:T(128)S(1)}, /*index=5*/f32[2048]{0:T(1024)...) while((s32[]{:T(128)}, f32[512]{0:T(512)S(1)}, ...), condition=%wide.region_12.13_spmd.clone, body=%wide.region_9.12_spmd.clone.sunk | while | flops 137101312 | bytes 1604829 | solution.py:112
  219.3 56.1 %psum.56 = f32[512]{0:T(512)S(1)} all-reduce(f32[512]{0:T(512)S(1)} %get-tuple-element.464), channel_id=1, replica_groups=mesh['row'=16,'col'=32] {'col'}, use_global_device_ids=true, to_apply=%region_13.14 | all-reduce | flops 512 | bytes 4096 | tf_op jit(solution)/shard_map/psum | solution.py:113
  275.5 51.8 %psum.57 = f32[2048]{0:T(1024)S(1)} all-reduce(f32[2048]{0:T(1024)S(1)} %bitcast.189), channel_id=1, replica_groups=mesh['row'=16,'col'=32] {'row'}, use_global_device_ids=true, to_apply=%region_14.15 | all-reduce | flops 2048 | bytes 16384 | tf_op jit(solution)/shard_map/psum | solution.py:114
  327.3 13.7 %while.102 = (s32[]{:T(128)}, f32[512]{0:T(512)S(1)}, f32[4,512]{1,0:T(4,128)S(1)}, s32[4]{0:T(128)S(1)}, f32[2048]{0:T(1024)S(1)}, /*index=5*/f32[512]{0:T(512)...) while((s32[]{:T(128)}, f32[512]{0:T(512)S(1)}, ...), condition=%wide.region_18.19_spmd.clone, body=%wide.region_15.18_spmd.clone.sunk | while | flops 137101312 | bytes 1604829 | solution.py:91
  341.0 24.0 %pmax.52 = f32[2048]{0:T(1024)S(1)} all-reduce(f32[2048]{0:T(1024)S(1)} %bitcast.190), channel_id=1, replica_groups=mesh['row'=16,'col'=32] {'row'}, use_global_device_ids=true, to_apply=%region_20.21 | all-reduce | flops 2048 | bytes 16384 | tf_op jit(solution)/shard_map/pmax | solution.py:95
  365.1 57.4 %pmax.51 = f32[512]{0:T(512)S(1)} all-reduce(f32[512]{0:T(512)S(1)} %get-tuple-element.466), channel_id=1, replica_groups=mesh['row'=16,'col'=32] {'col'}, use_global_device_ids=true, to_apply=%region_19.20 | all-reduce | flops 512 | bytes 4096 | tf_op jit(solution)/shard_map/pmax | solution.py:94
  422.5 14.9 %while.103 = (s32[]{:T(128)}, f32[512]{0:T(512)S(1)}, f32[4,512]{1,0:T(4,128)S(1)}, s32[4]{0:T(128)S(1)}, f32[2048]{0:T(1024)S(1)}, /*index=5*/f32[512]{0:T(512)...) while((s32[]{:T(128)}, f32[512]{0:T(512)S(1)}, ...), condition=%wide.region_24.25_spmd.clone, body=%wide.region_21.24_spmd.clone.sunk | while | flops 137625600 | bytes 1613041 | solution.py:112
  437.4 56.1 %psum.58 = f32[512]{0:T(512)S(1)} all-reduce(f32[512]{0:T(512)S(1)} %get-tuple-element.468), channel_id=1, replica_groups=mesh['row'=16,'col'=32] {'col'}, use_global_device_ids=true, to_apply=%region_25.26 | all-reduce | flops 512 | bytes 4096 | tf_op jit(solution)/shard_map/psum | solution.py:113
  493.6 51.8 %psum.59 = f32[2048]{0:T(1024)S(1)} all-reduce(f32[2048]{0:T(1024)S(1)} %bitcast.191), channel_id=1, replica_groups=mesh['row'=16,'col'=32] {'row'}, use_global_device_ids=true, to_apply=%region_26.27 | all-reduce | flops 2048 | bytes 16384 | tf_op jit(solution)/shard_map/psum | solution.py:114
  545.4 13.5 %while.104 = (s32[]{:T(128)}, f32[512]{0:T(512)S(1)}, f32[4,512]{1,0:T(4,128)S(1)}, s32[4]{0:T(128)S(1)}, f32[2048]{0:T(1024)S(1)}, /*index=5*/f32[512]{0:T(512)...) while((s32[]{:T(128)}, f32[512]{0:T(512)S(1)}, ...), condition=%wide.region_30.31_spmd.clone, body=%wide.region_27.30_spmd.clone.sunk | while | flops 137101312 | bytes 1604829 | solution.py:91
  558.8 24.1 %pmax.54 = f32[2048]{0:T(1024)S(1)} all-reduce(f32[2048]{0:T(1024)S(1)} %bitcast.192), channel_id=1, replica_groups=mesh['row'=16,'col'=32] {'row'}, use_global_device_ids=true, to_apply=%region_32.33 | all-reduce | flops 2048 | bytes 16384 | tf_op jit(solution)/shard_map/pmax | solution.py:95
  582.9 57.4 %pmax.53 = f32[512]{0:T(512)S(1)} all-reduce(f32[512]{0:T(512)S(1)} %get-tuple-element.470), channel_id=1, replica_groups=mesh['row'=16,'col'=32] {'col'}, use_global_device_ids=true, to_apply=%region_31.32 | all-reduce | flops 512 | bytes 4096 | tf_op jit(solution)/shard_map/pmax | solution.py:94
  640.3 15.5 %while.105 = (s32[]{:T(128)}, f32[512]{0:T(512)S(1)}, f32[4,512]{1,0:T(4,128)S(1)}, s32[4]{0:T(128)S(1)}, f32[2048]{0:T(1024)S(1)}, /*index=5*/f32[512]{0:T(512)...) while((s32[]{:T(128)}, f32[512]{0:T(512)S(1)}, ...), condition=%wide.region_36.37_spmd.clone, body=%wide.region_33.36_spmd.clone.sunk | while | flops 137625600 | bytes 1613041 | solution.py:112
  655.8 38.2 %psum.61 = f32[2048]{0:T(1024)S(1)} all-reduce(f32[2048]{0:T(1024)S(1)} %bitcast.193), channel_id=1, replica_groups=mesh['row'=16,'col'=32] {'row'}, use_global_device_ids=true, to_apply=%region_38.39 | all-reduce | flops 2048 | bytes 16384 | tf_op jit(solution)/shard_map/psum | solution.py:114
  707.3 55.7 %pmax.55 = f32[512]{0:T(512)S(1)} all-reduce(f32[512]{0:T(512)S(1)} %get-tuple-element.474), channel_id=1, replica_groups=mesh['row'=16,'col'=32] {'col'}, use_global_device_ids=true, to_apply=%region_42.43 | all-reduce | flops 512 | bytes 4096 | tf_op jit(solution)/shard_map/pmax | solution.py:94
  763.0 13.4 %while.107 = (s32[]{:T(128)}, f32[512]{0:T(512)S(1)}, s32[4]{0:T(128)S(1)}, f32[2048]{0:T(1024)S(1)}, f32[512]{0:T(512)S(1)}, /*index=5*/f32[2048]{0:T(1024)S(1)...) while((s32[]{:T(128)}, f32[512]{0:T(512)S(1)}, ...), condition=%wide.region_45.46_spmd.clone, body=%wide.region_43.45_spmd.clone.sunk | while | flops 136577536 | bytes 1598673 | solution.py:112
  776.4 57.7 %all-reduce.1 = (f32[512]{0:T(512)S(1)}, f32[512]{0:T(512)S(1)}) all-reduce(f32[512]{0:T(512)S(1)} %get-tuple-element.475, f32[512]{0:T(512)S(1)} %get-tuple-element.472), channel_id=1, replica_groups=mesh['row'=16,'col'=32] {'col'}, use_global_device_ids=true, to_apply=%region_46.47 | all-reduce | flops 1024 | bytes 8192 | tf_op jit(solution)/shard_map/psum | solution.py:113
  834.7 52.1 %psum.63 = f32[]{:T(128)} all-reduce(f32[]{:T(128)} %get-tuple-element.1210), channel_id=1, replica_groups=mesh['row'=16,'col'=32] {'row'}, use_global_device_ids=true, to_apply=%region_48.49 | all-reduce | flops 1 | bytes 8 | tf_op jit(solution)/shard_map/psum | solution.py:123
  (235 shorter events, 115.6 us)
Async XLA Ops:
  6.5 89.3 %all-gather.3.cloned.1.call-start = ((), (), s32[]{:S(2)}) async-start(), calls=%async_computation | async-start | bytes 1114112 | tf_op jit(solution)/shard_map/all_gather | solution.py:52
Sparse Core Ops, SparseCore 0:
  9.5 48.0 all-gather.2
where the time goes:
time: 897 us; the launch traced here: 895 us
  blocking collectives  757 us (84%)
  matrix products  68.1 us (8%)
  local copies, waits for them, and re-layouts  28.5 us (3%)
  loops' own time  21.2 us (2%)
  between operations  14.4 us (2%)
    pmax x4, blocking collectives, shards(): row_high = lax.pmax(row_local, 'col')  229 us
    psum x3, blocking collectives, shards(): row_sum = lax.psum(row_part, 'col')  170 us
    psum x3, blocking collectives, shards(): col_sum = lax.psum(col_part.reshape(col_count), 'row')  142 us
    pmax x3, blocking collectives, shards(): col_high = lax.pmax(col_local.reshape(col_count), 'row')  84.1 us
    dot_general x32, matrix products, inner_products(): lax.dot_general(left_rows, right_rows, (((1,), (1,)), ((), ())), preferre...  64 us
    psum x1, blocking collectives, shards(): potential_sum = lax.psum(jnp.sum(row_pot), 'row')  52.1 us
    all_gather x1, blocking collectives, shards(): lax.all_gather(train_embed, 'col', axis=0, tiled=True)  34.7 us
    all_gather x1, blocking collectives, shards(): lax.all_gather(valid_labels, 'row', axis=0, tiled=True)  28 us
  transfers between devices with their start and end apart: 1, of which 0 were waited for; matrix products, arithmetic and copies ran while one was open for 1% of the time, Pallas kernels for 0%

commit v1 on v0

--- a/solution.py
+++ b/solution.py
@@ -110,7 +110,11 @@
             )
 
         row_part, col_part = lax.scan(local_totals, jnp.zeros((row_count,), jnp.float32), block_ids)
-        row_sum = lax.psum(row_part, "col")
+        row_sum = row_part
+        for hop in (1, 2, 4, 8, 16):
+            row_sum = row_sum + lax.ppermute(
+                row_sum, "col", [(dev, dev ^ hop) for dev in range(32)]
+            )
         col_sum = lax.psum(col_part.reshape(col_count), "row")
         row_new = entropy_scale * math.log(full_cols) - entropy_scale * (
             row_high + jnp.log(row_sum)

time: 897 us -> 784 us (0.87)
  blocking collectives: 757 us -> 560 us
  starting transfers between devices: 0.01 us -> 56 us
  waiting for transfers between devices: 0.71 us -> 28.1 us
    psum x3 -> x0, blocking collectives: 170 us -> none  [shards(): row_sum = lax.psum(row_part, 'col')]
    ppermute x0 -> x20, starting transfers between devices: none -> 56 us  [shards(): lax.ppermute(row_sum, 'col', [(dev, dev ^ hop) for dev in range(32)])]
    ppermute x0 -> x20, waiting for transfers between devices: none -> 27.4 us  [shards(): lax.ppermute(row_sum, 'col', [(dev, dev ^ hop) for dev in range(32)])]
    psum x3, blocking collectives: 142 us -> 122 us  [shards(): col_sum = lax.psum(col_part.reshape(col_count), 'row')]
    psum x1, blocking collectives: 52.1 us -> 41.6 us  [shards(): potential_sum = lax.psum(jnp.sum(row_pot), 'row')]
  transfers between devices with their start and end apart: 1 -> 21, of which waited for: 0 -> 10; matrix products, arithmetic and copies ran while one was open for 1% -> 4% of each run, Pallas kernels for 0% -> 0%
where the time goes in v1:
time: 784 us; the launch traced here: 782 us
  blocking collectives  560 us (71%)
  matrix products  68.1 us (9%)
  starting transfers between devices  56 us (7%)
  local copies, waits for them, and re-layouts  28.6 us (4%)
  waiting for transfers between devices  28.1 us (4%)
  loops' own time  21.4 us (3%)
  between operations  14.7 us (2%)
    pmax x4, blocking collectives, shards(): row_high = lax.pmax(row_local, 'col')  230 us
    psum x3, blocking collectives, shards(): col_sum = lax.psum(col_part.reshape(col_count), 'row')  122 us
    pmax x3, blocking collectives, shards(): col_high = lax.pmax(col_local.reshape(col_count), 'row')  86.4 us
    dot_general x32, matrix products, inner_products(): lax.dot_general(left_rows, right_rows, (((1,), (1,)), ((), ())), preferre...  64 us
    ppermute x20, starting transfers between devices, shards(): lax.ppermute(row_sum, 'col', [(dev, dev ^ hop) for dev in range(32)])  56 us
    psum x1, blocking collectives, shards(): potential_sum = lax.psum(jnp.sum(row_pot), 'row')  41.6 us
    all_gather x1, blocking collectives, shards(): lax.all_gather(train_embed, 'col', axis=0, tiled=True)  34.7 us
    all_gather x1, blocking collectives, shards(): lax.all_gather(valid_labels, 'row', axis=0, tiled=True)  28 us
  transfers between devices with their start and end apart: 21, of which 10 were waited for; matrix products, arithmetic and copies ran while one was open for 4% of the time, Pallas kernels for 0%

profile of v1, /device:TPU:1, one launch (start us, length us, event | category | flops | bytes accessed | tf_op | source)
XLA Modules:
  0.0 782.3 jit_solution(4030312618932380438)
XLA Ops:
  10.2 17.5 %all-reduce = s32[512]{0:T(512)S(1)} all-reduce(s32[512]{0:T(512)S(1)} %dynamic-update-slice), channel_id=1, replica_groups=mesh['row'=16,'col'=32] {'col'}, use_global_device_ids=true, to_apply=%add | all-reduce | flops 512 | bytes 4096
  27.7 28.0 %all-gather = s32[16,1,128]{2,1,0:T(1,128)S(1)} all-gather(s32[1,1,128]{2,1,0:T(1,128)} %bitcast.194), channel_id=1, replica_groups=mesh['row'=16,'col'=32] {'row'}, dimensions={0}, use_global_device_ids=true | all-gather | bytes 8704 | tf_op jit(solution)/shard_map/all_gather | solution.py:53
  55.7 34.7 %all_gather.12 = bf16[512,256]{1,0:T(8,128)(2,1)S(1)} all-gather(bf16[16,256]{1,0:T(8,128)(2,1)} %param.22), channel_id=1, replica_groups=mesh['row'=16,'col'=32] {'col'}, dimensions={0}, use_global_device_ids=true | all-gather | bytes 270336 | tf_op jit(solution)/shard_map/all_gather | solution.py:39
  97.4 13.4 %while.100 = (s32[]{:T(128)}, f32[512]{0:T(512)S(1)}, f32[4,512]{1,0:T(4,128)S(1)}, f32[512]{0:T(512)S(1)}, s32[4]{0:T(128)S(1)}, /*index=5*/f32[2048]{0:T(1024)...) while((s32[]{:T(128)}, f32[512]{0:T(512)S(1)}, ...), condition=%wide.region_6.7_spmd.clone, body=%wide.region_3.6_spmd.clone.sunk | while | flops 136577024 | bytes 1596617 | solution.py:91
  110.8 36.0 %pmax.50 = f32[2048]{0:T(1024)S(1)} all-reduce(f32[2048]{0:T(1024)S(1)} %bitcast.190), channel_id=1, replica_groups=mesh['row'=16,'col'=32] {'row'}, use_global_device_ids=true, to_apply=%region_8.9 | all-reduce | flops 2048 | bytes 16384 | tf_op jit(solution)/shard_map/pmax | solution.py:95
  146.8 58.1 %pmax.49 = f32[512]{0:T(512)S(1)} all-reduce(f32[512]{0:T(512)S(1)} %get-tuple-element.462), channel_id=1, replica_groups=mesh['row'=16,'col'=32] {'col'}, use_global_device_ids=true, to_apply=%region_7.8 | all-reduce | flops 512 | bytes 4096 | tf_op jit(solution)/shard_map/pmax | solution.py:94
  204.9 14.4 %while.101 = (s32[]{:T(128)}, f32[512]{0:T(512)S(1)}, f32[4,512]{1,0:T(4,128)S(1)}, f32[512]{0:T(512)S(1)}, s32[4]{0:T(128)S(1)}, /*index=5*/f32[2048]{0:T(1024)...) while((s32[]{:T(128)}, f32[512]{0:T(512)S(1)}, ...), condition=%wide.region_12.13_spmd.clone, body=%wide.region_9.12_spmd.clone.sunk | while | flops 137101312 | bytes 1604829 | solution.py:112
  235.7 41.7 %psum.28 = f32[2048]{0:T(1024)S(1)} all-reduce(f32[2048]{0:T(1024)S(1)} %bitcast.182), channel_id=1, replica_groups=mesh['row'=16,'col'=32] {'row'}, use_global_device_ids=true, to_apply=%region_13.14 | all-reduce | flops 2048 | bytes 16384 | tf_op jit(solution)/shard_map/psum | solution.py:118
  277.4 5.9 collective-permute-start.4
  285.7 13.9 %while.102 = (s32[]{:T(128)}, f32[512]{0:T(512)S(1)}, f32[4,512]{1,0:T(4,128)S(1)}, s32[4]{0:T(128)S(1)}, f32[2048]{0:T(1024)S(1)}, /*index=5*/f32[512]{0:T(512)...) while((s32[]{:T(128)}, f32[512]{0:T(512)S(1)}, ...), condition=%wide.region_17.18_spmd.clone, body=%wide.region_14.17_spmd.clone.sunk | while | flops 137101312 | bytes 1604829 | solution.py:91
  299.6 25.2 %pmax.52 = f32[2048]{0:T(1024)S(1)} all-reduce(f32[2048]{0:T(1024)S(1)} %bitcast.191), channel_id=1, replica_groups=mesh['row'=16,'col'=32] {'row'}, use_global_device_ids=true, to_apply=%region_19.20 | all-reduce | flops 2048 | bytes 16384 | tf_op jit(solution)/shard_map/pmax | solution.py:95
  324.8 57.4 %pmax.51 = f32[512]{0:T(512)S(1)} all-reduce(f32[512]{0:T(512)S(1)} %get-tuple-element.466), channel_id=1, replica_groups=mesh['row'=16,'col'=32] {'col'}, use_global_device_ids=true, to_apply=%region_18.19 | all-reduce | flops 512 | bytes 4096 | tf_op jit(solution)/shard_map/pmax | solution.py:94
  382.2 15.0 %while.103 = (s32[]{:T(128)}, f32[512]{0:T(512)S(1)}, f32[4,512]{1,0:T(4,128)S(1)}, s32[4]{0:T(128)S(1)}, f32[2048]{0:T(1024)S(1)}, /*index=5*/f32[512]{0:T(512)...) while((s32[]{:T(128)}, f32[512]{0:T(512)S(1)}, ...), condition=%wide.region_23.24_spmd.clone, body=%wide.region_20.23_spmd.clone.sunk | while | flops 137625600 | bytes 1613041 | solution.py:112
  413.6 41.7 %psum.29 = f32[2048]{0:T(1024)S(1)} all-reduce(f32[2048]{0:T(1024)S(1)} %bitcast.183), channel_id=1, replica_groups=mesh['row'=16,'col'=32] {'row'}, use_global_device_ids=true, to_apply=%region_24.25 | all-reduce | flops 2048 | bytes 16384 | tf_op jit(solution)/shard_map/psum | solution.py:118
  463.6 13.4 %while.104 = (s32[]{:T(128)}, f32[512]{0:T(512)S(1)}, f32[4,512]{1,0:T(4,128)S(1)}, s32[4]{0:T(128)S(1)}, f32[2048]{0:T(1024)S(1)}, /*index=5*/f32[512]{0:T(512)...) while((s32[]{:T(128)}, f32[512]{0:T(512)S(1)}, ...), condition=%wide.region_28.29_spmd.clone, body=%wide.region_25.28_spmd.clone.sunk | while | flops 137101312 | bytes 1604829 | solution.py:91
  477.0 25.2 %pmax.54 = f32[2048]{0:T(1024)S(1)} all-reduce(f32[2048]{0:T(1024)S(1)} %bitcast.192), channel_id=1, replica_groups=mesh['row'=16,'col'=32] {'row'}, use_global_device_ids=true, to_apply=%region_30.31 | all-reduce | flops 2048 | bytes 16384 | tf_op jit(solution)/shard_map/pmax | solution.py:95
  502.3 57.4 %pmax.53 = f32[512]{0:T(512)S(1)} all-reduce(f32[512]{0:T(512)S(1)} %get-tuple-element.470), channel_id=1, replica_groups=mesh['row'=16,'col'=32] {'col'}, use_global_device_ids=true, to_apply=%region_29.30 | all-reduce | flops 512 | bytes 4096 | tf_op jit(solution)/shard_map/pmax | solution.py:94
  559.7 15.5 %while.105 = (s32[]{:T(128)}, f32[512]{0:T(512)S(1)}, f32[4,512]{1,0:T(4,128)S(1)}, s32[4]{0:T(128)S(1)}, f32[2048]{0:T(1024)S(1)}, /*index=5*/f32[512]{0:T(512)...) while((s32[]{:T(128)}, f32[512]{0:T(512)S(1)}, ...), condition=%wide.region_34.35_spmd.clone, body=%wide.region_31.34_spmd.clone.sunk | while | flops 137625600 | bytes 1613041 | solution.py:112
  577.1 38.2 %psum.30 = f32[2048]{0:T(1024)S(1)} all-reduce(f32[2048]{0:T(1024)S(1)} %bitcast.193), channel_id=1, replica_groups=mesh['row'=16,'col'=32] {'row'}, use_global_device_ids=true, to_apply=%region_35.36 | all-reduce | flops 2048 | bytes 16384 | tf_op jit(solution)/shard_map/psum | solution.py:118
  615.4 13.1 %while.106 = (s32[]{:T(128)}, f32[512]{0:T(512)S(1)}, s32[4]{0:T(128)S(1)}, f32[2048]{0:T(1024)S(1)}, f32[512]{0:T(512)S(1)}, /*index=5*/f32[2048]{0:T(1024)S(1)...) while((s32[]{:T(128)}, f32[512]{0:T(512)S(1)}, ...), condition=%wide.region_38.39_spmd.clone, body=%wide.region_36.38_spmd.clone.sunk | while | flops 136315392 | bytes 1596617 | solution.py:91
  628.5 57.4 %pmax.55 = f32[512]{0:T(512)S(1)} all-reduce(f32[512]{0:T(512)S(1)} %get-tuple-element.474), channel_id=1, replica_groups=mesh['row'=16,'col'=32] {'col'}, use_global_device_ids=true, to_apply=%region_39.40 | all-reduce | flops 512 | bytes 4096 | tf_op jit(solution)/shard_map/pmax | solution.py:94
  686.0 13.4 %while.107 = (s32[]{:T(128)}, f32[512]{0:T(512)S(1)}, s32[4]{0:T(128)S(1)}, f32[2048]{0:T(1024)S(1)}, f32[512]{0:T(512)S(1)}, /*index=5*/f32[2048]{0:T(1024)S(1)...) while((s32[]{:T(128)}, f32[512]{0:T(512)S(1)}, ...), condition=%wide.region_42.43_spmd.clone, body=%wide.region_40.42_spmd.clone.sunk | while | flops 136577536 | bytes 1598673 | solution.py:112
  723.7 5.2 collective-permute-start.19
  732.6 41.6 %psum.31 = f32[]{:T(128)} all-reduce(f32[]{:T(128)} %get-tuple-element.1208), channel_id=1, replica_groups=mesh['row'=16,'col'=32] {'row'}, use_global_device_ids=true, to_apply=%region_44.45 | all-reduce | flops 1 | bytes 8 | tf_op jit(solution)/shard_map/psum | solution.py:127
  (288 shorter events, 174.8 us)
Async XLA Ops:
  6.5 89.2 %all-gather.3.cloned.1.call-start = ((), (), s32[]{:S(2)}) async-start(), calls=%async_computation | async-start | bytes 1114112 | tf_op jit(solution)/shard_map/all_gather | solution.py:52
  219.3 4.3 collective-permute-start
  223.7 5.8 collective-permute-start.1
  229.5 4.3 collective-permute-start.2
  233.8 43.6 %collective-permute-start.3 = (f32[512]{0:T(512)S(1)}, f32[512]{0:T(512)S(1)}, u32[]{:S(2)}, u32[]{:S(2)}) collective-permute-start(f32[512]{0:T(512)S(1)} %add.319), channel_id=1, source_target_pairs={{0,8},{1,9},{2,10},{3,11},{4,12},{5,13},{6,14},{7,15},{8,0},{9,1},... | collective-permute-start | bytes 6152 | tf_op jit(solution)/shard_map/ppermute | solution.py:115
  277.4 8.2 %collective-permute-start.4 = (f32[512]{0:T(512)S(1)}, f32[512]{0:T(512)S(1)}, u32[]{:S(2)}, u32[]{:S(2)}) collective-permute-start(f32[512]{0:T(512)S(1)} %add.320), channel_id=1, source_target_pairs={{0,16},{1,17},{2,18},{3,19},{4,20},{5,21},{6,22},{7,23},{8,24},{9,... | collective-permute-start | bytes 6152 | tf_op jit(solution)/shard_map/ppermute | solution.py:115
  397.2 4.3 collective-permute-start.5
  401.5 5.8 collective-permute-start.6
  407.3 4.3 collective-permute-start.7
  411.7 43.6 %collective-permute-start.8 = (f32[512]{0:T(512)S(1)}, f32[512]{0:T(512)S(1)}, u32[]{:S(2)}, u32[]{:S(2)}) collective-permute-start(f32[512]{0:T(512)S(1)} %add.326), channel_id=1, source_target_pairs={{0,8},{1,9},{2,10},{3,11},{4,12},{5,13},{6,14},{7,15},{8,0},{9,1},... | collective-permute-start | bytes 6152 | tf_op jit(solution)/shard_map/ppermute | solution.py:115
  455.3 8.2 %collective-permute-start.9 = (f32[512]{0:T(512)S(1)}, f32[512]{0:T(512)S(1)}, u32[]{:S(2)}, u32[]{:S(2)}) collective-permute-start(f32[512]{0:T(512)S(1)} %add.327), channel_id=1, source_target_pairs={{0,16},{1,17},{2,18},{3,19},{4,20},{5,21},{6,22},{7,23},{8,24},{9,... | collective-permute-start | bytes 6152 | tf_op jit(solution)/shard_map/ppermute | solution.py:115
  575.2 126.1 %collective-permute-start.10 = (f32[512]{0:T(512)S(1)}, f32[512]{0:T(512)S(1)}, u32[]{:S(2)}, u32[]{:S(2)}) collective-permute-start(f32[512]{0:T(512)S(1)} %get-tuple-element.472), channel_id=1, source_target_pairs={{0,1},{1,0},{2,3},{3,2},{4,5},{5,4},{6,7},{7,6},{8,9},{9,8},{10,11... | collective-permute-start | bytes 6152 | tf_op jit(solution)/shard_map/ppermute | solution.py:115
  699.4 4.3 collective-permute-start.15
  701.3 6.8 collective-permute-start.11
  703.7 6.4 collective-permute-start.16
  708.2 5.3 collective-permute-start.12
  710.1 5.3 collective-permute-start.17
  713.5 6.2 collective-permute-start.13
  715.5 8.2 %collective-permute-start.18 = (f32[512]{0:T(512)S(1)}, f32[512]{0:T(512)S(1)}, u32[]{:S(2)}, u32[]{:S(2)}) collective-permute-start(f32[512]{0:T(512)S(1)} %add.344), channel_id=1, source_target_pairs={{0,8},{1,9},{2,10},{3,11},{4,12},{5,13},{6,14},{7,15},{8,0},{9,1},... | collective-permute-start | bytes 6152 | tf_op jit(solution)/shard_map/ppermute | solution.py:115
  719.8 9.2 %collective-permute-start.14 = (f32[512]{0:T(512)S(1)}, f32[512]{0:T(512)S(1)}, u32[]{:S(2)}, u32[]{:S(2)}) collective-permute-start(f32[512]{0:T(512)S(1)} %add.336), channel_id=1, source_target_pairs={{0,16},{1,17},{2,18},{3,19},{4,20},{5,21},{6,22},{7,23},{8,24},{9,... | collective-permute-start | bytes 6152 | tf_op jit(solution)/shard_map/ppermute | solution.py:115
  723.7 8.2 %collective-permute-start.19 = (f32[512]{0:T(512)S(1)}, f32[512]{0:T(512)S(1)}, u32[]{:S(2)}, u32[]{:S(2)}) collective-permute-start(f32[512]{0:T(512)S(1)} %add.345), channel_id=1, source_target_pairs={{0,16},{1,17},{2,18},{3,19},{4,20},{5,21},{6,22},{7,23},{8,24},{9,... | collective-permute-start | bytes 6152 | tf_op jit(solution)/shard_map/ppermute | solution.py:115
Sparse Core Ops, SparseCore 0:
  9.5 47.9 all-gather.2
